TPU v7x, 32 devices: a whole 2x2x4 slice. The times are simulated.
32 devices in a mesh: px: 4 (over y, core), py: 8 (over z, x).
Axes of the slice: x: 2, y: 2, z: 4, core: 2. Of those that a mesh axis runs over, the one named last changes fastest.
Arguments:
- source: float32 [128, 128, 256], P('px', 'py'), may hold values from -3.5 to 3.7
- density: float32 [128, 128, 256], P('px', 'py'), may hold values from 0.25 to 4
Outputs:
- pressure: float32 [128, 128, 256], P('px', 'py')
All inputs are finite; a program needn't handle non-finite values.
Results may differ from a plain program's by a relative error of at most 0.0001.
Values sent between devices are 32-bit elements; how exact they have to be, the bound alone decides.
A program may use at most 128 MiB of HBM per device.

v0:
```python
import functools

import jax
import jax.numpy as jnp
from jax import lax
from jax.experimental import pallas as pl
from jax.experimental.pallas import tpu as pltpu
from jax.sharding import PartitionSpec as P

COARSE = 8
LANES = 128
HX0, HX1, HY, PAD2 = 4, 4, 4, 2
THREE, TWO = ((0, 2), (2, 1)), ((0, 2),)
ROWS = 8
DIRECTIONS = [(dx, dy) for dx in (-1, 0, 1) for dy in (-1, 0, 1) if (dx, dy) != (0, 0)]
MESH = pl.DeviceIdType.MESH


def iota(shape, dim):
    return lax.broadcasted_iota(jnp.int32, shape, dim)


def dot(a, b):
    return jnp.dot(a, b, precision=lax.Precision.HIGHEST, preferred_element_type=jnp.float32)


def matrix(shape, test, value):
    return jnp.where(test(iota(shape, 0), iota(shape, 1)), value, 0.0).astype(jnp.float32)


def loop(low, high, body, unroll=1):
    def step(i, carry):
        body(i)
        return carry

    lax.fori_loop(low, high, step, 0, unroll=unroll)


def chunks(low, high, size, most, body):
    count = high - low
    n = max(d for d in range(1, count + 1) if count % d == 0 and (d == 1 or d * size <= most))
    if n == count:
        body(low, n)
    else:
        loop(0, count // n, lambda i: body(low + i * n, n))


class Level:
    def __init__(self, refs, factor, start, total, rows, lanes, span, packed):
        (self.m, self.wx, self.wy, self.wz, self.k, self.g, self.u) = refs
        self.low, self.high = span
        self.half = 0.5 * factor
        self.start, self.total = start, total
        shape = self.m.shape[1:]
        self.shape, self.packed = shape, packed
        row, lane = iota(shape, 0), iota(shape, 1)
        first, total_y = rows
        nz, stride = lanes
        group = lane // stride if packed else 0
        gy = row + group * shape[0]
        if not packed:
            gy = first + jnp.where(row < shape[0] - HY, row, row - shape[0])
        gz = lane % stride if packed else lane
        self.row = row
        self.size = -(-shape[0] // ROWS) * (shape[1] // LANES)

        def keep(pos, count, span):
            plus = (pos != count - 1) & (pos != -1) & (pos != span - 1)
            minus = (pos != 0) & (pos != count)
            return jnp.where(plus, 1.0, 0.0), jnp.where(minus, 1.0, 0.0)

        self.kyp, self.kym = keep(gy, total_y, -9)
        self.kzp, self.kzm = keep(gz, nz, stride)
        self.gz, self.nz = gz, nz

    def y_minus(self, t):
        r = pltpu.roll(t, 1, t.ndim - 2)
        if self.packed:
            r = jnp.where(self.row == 0, pltpu.roll(r, LANES // 2, r.ndim - 1), r)
        return r

    def y_plus(self, t):
        r = pltpu.roll(t, self.shape[0] - 1, t.ndim - 2)
        if self.packed:
            r = jnp.where(self.row == self.shape[0] - 1, pltpu.roll(r, LANES // 2, r.ndim - 1), r)
        return r

    def z_minus(self, t):
        return pltpu.roll(t, 1, t.ndim - 1)

    def z_plus(self, t):
        return pltpu.roll(t, self.shape[1] - 1, t.ndim - 1)

    def clear(self, *refs):
        for i in (self.low - 1, self.high):
            for ref in refs:
                ref[i] = jnp.zeros(self.shape, jnp.float32)

    def face(self, x):
        gx = self.start + x
        return jnp.where((gx != self.total - 1) & (gx != -1), 1.0, 0.0)

    def setup(self, source=None):
        before = self.low - 1
        self.wx[before] = (self.half * self.face(before)) * (self.m[before] + self.m[self.low])
        known = self.kyp + self.kym + self.kzp + self.kzm

        def body(x, n):
            m = [self.m[x - 1 + j] for j in range(n + 2)]
            f = None if source is None else [source(x + j) for j in range(n)]
            k = [self.face(x - 1 + j) for j in range(n + 1)]
            s = [k[j] * (m[j] + m[j + 1]) for j in range(n + 1)]
            done = []
            for j in range(n):
                c = m[j + 1]
                wyp = self.kyp * (c + self.y_plus(c))
                wym = self.kym * (c + self.y_minus(c))
                wzp = self.kzp * (c + self.z_plus(c))
                wzm = self.kzm * (c + self.z_minus(c))
                missing = 6.0 - (k[j] + k[j + 1]) - known
                diag = ((s[j] + s[j + 1]) + (wyp + wym)) + ((wzp + wzm) + 2.0 * c * missing)
                done.append((self.half * s[j + 1], self.half * wyp, self.half * wzp,
                             0.8 / (self.half * diag)))
            for j, (wx, wy, wz, inverse) in enumerate(done):
                self.wx[x + j] = wx
                self.wy[x + j] = wy
                self.wz[x + j] = wz
                self.k[x + j] = inverse
                if f is not None:
                    self.g[x + j] = inverse * f[j]

        chunks(self.low, self.high, self.size, 12, body)

    def scale(self):
        def body(x, n):
            at = pl.ds(x, n)
            self.g[at] = self.k[at] * self.g[at]

        chunks(self.low, self.high, self.size, 24, body)

    def change(self, ref, x, n):
        at = pl.ds(x, n)
        v, wy, wz = ref[at], self.wy[at], self.wz[at]
        total = self.wx[at] * ref[pl.ds(x + 1, n)] + self.wx[pl.ds(x - 1, n)] * ref[pl.ds(x - 1, n)]
        total = total + (wy * self.y_plus(v) + self.y_minus(wy * v))
        total = total + (wz * self.z_plus(v) + self.z_minus(wz * v))
        return v, self.g[at] + self.k[at] * total

    def sweep(self, src, dst, inset=0):
        def body(x, n):
            v, rest = self.change(src, x, n)
            dst[pl.ds(x, n)] = 0.2 * v + rest

        chunks(self.low + inset, self.high - inset, self.size, 24, body)

    def residual(self, x, n):
        v, rest = self.change(self.u, x, n)
        return (rest - 0.8 * v) / self.k[pl.ds(x, n)]


def columns(width):
    return [slice(c, c + LANES) for c in range(0, width, LANES)]


def pair_slabs(tmp, i, value):
    count, rows, width = value.shape
    sums = [value[j] + value[j + 1] for j in range(0, count, 2)]
    for j, both in enumerate(sums):
        for k, c in enumerate(columns(width)):
            tmp[k, i + j, 0:rows] = both[:, c]


def pair_rows(tmp, count, rows, width):
    parts = [
        tmp[k, 0:count, pl.ds(0, rows, stride=2)] + tmp[k, 0:count, pl.ds(1, rows, stride=2)]
        for k in range(width // LANES)
    ]
    return parts[0] if len(parts) == 1 else jnp.concatenate(parts, 2)


def add_double(tmp, values, target, first, size):
    rows = 0
    for value in values:
        count, more, width = value.shape
        for k, c in enumerate(columns(width)):
            tmp[k, 0:count, pl.ds(2 * rows, more, stride=2)] = value[:, :, c]
            tmp[k, 0:count, pl.ds(2 * rows + 1, more, stride=2)] = value[:, :, c]
        rows += more

    def body(i, n):
        parts = [tmp[k, pl.ds(i, n), 0 : 2 * rows] for k in range(width // LANES)]
        e = parts[0] if len(parts) == 1 else jnp.concatenate(parts, 2)
        old = target[pl.ds(first + 2 * i, 2 * n)]
        new = [old[j] + e[j // 2] for j in range(2 * n)]
        for j in range(2 * n):
            target[first + 2 * i + j] = new[j]

    chunks(0, count, 2 * size, 24, body)


def kernel(sizes, source, density, out, den, src, l0, l1, l2, l3, pe0, pe1, t1, tmp,
           gm, gf, copy_sem, halos, sa, ra, sb, rb):
    px_count, py_count = sizes
    px, py = lax.axis_index("px"), lax.axis_index("py")
    bx, by, nz = source.shape
    nx, ny = bx * px_count, by * py_count
    bx1, by1, bx2, by2 = bx // 2, by // 2, bx // 4, by // 4

    def inside(dx, dy):
        test = None
        for d, pos, count in ((dx, px, px_count), (dy, py, py_count)):
            if d:
                one = (pos < count - 1) if d > 0 else (pos > 0)
                test = one if test is None else test & one
        return test

    class Halo:
        def __init__(self, refs, hx, pieces, block):
            self.xsend, self.xland, self.ysend, self.yland, self.send, self.recv = refs
            self.hx, self.pieces, self.block = hx, pieces, block

        def fill(self, value):
            edges = ((px == 0, 0, 0), (px == px_count - 1, 0, 1),
                     (py == 0, 1, 0), (py == py_count - 1, 1, 1))
            hx, bx = self.hx, self.block[0]
            for test, dim, side in edges:
                @pl.when(test)
                def _():
                    if dim == 0:
                        ref = self.xland
                        ref[side] = jnp.full(ref.shape[1:], value, jnp.float32)
                    for ref in self.yland:
                        if dim:
                            ref[side] = jnp.full(ref.shape[1:], value, jnp.float32)
                        else:
                            at = side * (hx + bx)
                            for s in range(2):
                                ref[s, at : at + hx] = jnp.full((hx,) + ref.shape[2:], value, jnp.float32)

        def pack(self, ref, ox):
            hx, (bx, by) = self.hx, self.block
            self.xsend[0] = ref[ox : ox + hx, 0:by]
            self.xsend[1] = ref[ox + bx - hx : ox + bx, 0:by]
            for ysend, (d, w) in zip(self.ysend, self.pieces):
                ysend[0] = ref[ox : ox + bx, d : d + w]
                ysend[1] = ref[ox : ox + bx, by - d - w : by - d]

        def each(self, act, sign):
            hx, bx = self.hx, self.block[0]
            n = 0
            for dx, dy in DIRECTIONS:
                if dy == 0:
                    side = (dx + 1) // 2
                    pairs = [(self.xsend.at[side], self.xland.at[1 - side])]
                else:
                    side = (dy + 1) // 2
                    own, there, count = ((0, hx + bx, hx), (0, hx, bx), (bx - hx, 0, hx))[dx + 1]
                    pairs = [
                        (a.at[side, pl.ds(own, count)], b.at[1 - side, pl.ds(there, count)])
                        for a, b in zip(self.ysend, self.yland)
                    ]
                copies = []
                for a, b in pairs:
                    copies.append(pltpu.make_async_remote_copy(
                        src_ref=a,
                        dst_ref=b,
                        send_sem=self.send.at[n],
                        recv_sem=self.recv.at[n],
                        device_id=(px + dx, py + dy),
                        device_id_type=MESH,
                    ))
                    n += 1

                @pl.when(inside(sign * dx, sign * dy))
                def _():
                    for copy in copies:
                        act(copy)

        def start(self):
            self.each(lambda c: c.start(), 1)

        def arrive(self):
            self.each(lambda c: c.wait_recv(), -1)

        def sent(self):
            self.each(lambda c: c.wait_send(), 1)

        def unpack(self, ref, ox, change=lambda v: v):
            hx, (bx, by), rows = self.hx, self.block, ref.shape[1]
            ref[ox - hx : ox, 0:by] = change(self.xland[0])
            ref[ox + bx : ox + bx + hx, 0:by] = change(self.xland[1])
            for yland, (d, w) in zip(self.yland, self.pieces):
                ref[ox - hx : ox + bx + hx, rows - d - w : rows - d] = change(yland[0])
                ref[ox - hx : ox + bx + hx, by + d : by + d + w] = change(yland[1])

    def along(axis, ref, send, recv, base):
        count, me = (py_count, py) if axis else (px_count, px)
        region = ref.at[px, py] if axis else ref.at[px]

        def each(act):
            for k in range(1, count):
                to = lax.rem(me + k, count)
                act(pltpu.make_async_remote_copy(
                    src_ref=region,
                    dst_ref=region,
                    send_sem=send.at[base + k - 1],
                    recv_sem=recv.at[base + k - 1],
                    device_id=(px, to) if axis else (to, py),
                    device_id_type=MESH,
                ))

        def arrive():
            for k in range(1, count):
                frm = lax.rem(me + count - k, count)
                landed = ref.at[px, frm] if axis else ref.at[frm]
                pltpu.make_async_remote_copy(
                    src_ref=landed,
                    dst_ref=landed,
                    send_sem=send.at[base + k - 1],
                    recv_sem=recv.at[base + k - 1],
                    device_id=(px, frm) if axis else (frm, py),
                    device_id_type=MESH,
                ).wait_recv()

        return (lambda: each(lambda c: c.start())), arrive, (lambda: each(lambda c: c.wait_send()))

    m0, f0, u0 = l0[0], l0[5], l0[6]
    m1, f1, u1 = l1[0], l1[5], l1[6]
    own_copies = [
        pltpu.make_async_copy(a, b, copy_sem.at[i])
        for i, (a, b) in enumerate(((density, den), (source, src)))
    ]
    for c in own_copies:
        c.start()
    block0, block1 = (bx, by), (bx1, by1)
    halo_m0 = Halo(halos[0], 3, THREE, block0)
    halo_f0 = Halo(halos[1], 2, TWO, block0)
    halo_u0 = Halo(halos[2], 2, TWO, block0)
    halo_m1 = Halo(halos[3], 3, THREE, block1)
    halo_f1 = Halo(halos[4], 2, TWO, block1)
    halo_u1 = Halo(halos[5], 3, THREE, block1)
    all_halos = (halo_m0, halo_f0, halo_u0, halo_m1, halo_f1, halo_u1)
    for h, value in zip(all_halos, (1.0, 0.0, 0.0, 1.0, 0.0, 0.0)):
        h.fill(value)

    barrier = pltpu.get_barrier_semaphore()
    for k in range(1, py_count):
        pl.semaphore_signal(barrier, 1, device_id=(px, lax.rem(py + k, py_count)), device_id_type=MESH)
    for k in range(1, px_count):
        pl.semaphore_signal(barrier, 1, device_id=(lax.rem(px + k, px_count), py), device_id_type=MESH)
    for dx, dy in DIRECTIONS:
        if dx and dy:
            @pl.when(inside(dx, dy))
            def _():
                pl.semaphore_signal(barrier, 1, device_id=(px + dx, py + dy), device_id_type=MESH)
    beside_x = jnp.minimum(px, 1) + jnp.minimum(px_count - 1 - px, 1)
    beside_y = jnp.minimum(py, 1) + jnp.minimum(py_count - 1 - py, 1)
    own_copies[0].wait()
    halo_m0.pack(den, 0)
    pl.semaphore_wait(barrier, px_count + py_count - 2 + beside_x * beside_y)

    halo_m0.start()
    own_copies[1].wait()
    halo_f0.pack(src, 0)
    halo_f0.start()

    r_fine = matrix((nz, LANES), lambda z, c: z // 2 == c, 0.125)
    r_low = matrix((LANES, LANES), lambda z, c: z // 2 == c, 0.125)
    r_high = matrix((LANES, LANES), lambda z, c: z // 2 + LANES // 2 == c, 0.125)
    half = LANES // 2
    r_pack = matrix(
        (LANES, LANES), lambda z, c: (z // half == c // half) & ((z % half) // 2 == c % half), 0.125
    )

    def restrict0(get, dst):
        def body(i, n):
            pair_slabs(tmp, i, get(HX0 + 2 * i, 2 * n))

        chunks(0, bx1, 2 * (y0 // ROWS) * (nz // LANES), 24, body)
        value = dot(pair_rows(tmp, bx1, by1, nz).reshape(bx1 * by1, nz), r_fine)
        dst[HX1 : HX1 + bx1, 0:by1] = value.reshape(bx1, by1, LANES)

    def restrict1(get, dst):
        def body(i, n):
            pair_slabs(tmp, i, get(HX1 + 2 * i, 2 * n))

        chunks(0, bx2, 2 * (y1 // ROWS), 24, body)
        sums = pair_rows(tmp, bx2, by2, LANES)
        for i in range(bx2):
            t1[i * by2 : (i + 1) * by2] = sums[i]
        n = bx2 * by2 // 2
        dst[px, py] = dot(t1[0:n], r_low) + dot(t1[n : 2 * n], r_high)

    wide0, wide1, wide2, wide3 = (l[0].shape[0] for l in (l0, l1, l2, l3))
    y0, y1 = l0[0].shape[1], l1[0].shape[1]

    def own(x, n):
        m0[pl.ds(HX0 + x, n), 0:by] = 1.0 / den[pl.ds(x, n)]
        f0[pl.ds(HX0 + x, n), 0:by] = src[pl.ds(x, n)]

    chunks(0, bx, (by // ROWS) * (nz // LANES), 24, own)
    restrict0(lambda x, n: m0[pl.ds(x, n), 0:by], m1)
    halo_m1.pack(m1, HX1)
    halo_m1.start()
    restrict1(lambda x, n: m1[pl.ds(x, n), 0:by1], gm)
    ma_start, ma_arrive, ma_sent = along(1, gm, sa, ra, 0)
    fa_start, fa_arrive, fa_sent = along(1, gf, sa, ra, py_count - 1)
    mb_start, mb_arrive, mb_sent = along(0, gm, sb, rb, 0)
    fb_start, fb_arrive, fb_sent = along(0, gf, sb, rb, px_count - 1)
    ma_start()

    level0 = Level(l0, 1.0, px * bx - HX0, nx, (py * by, ny), (nz, nz), (HX0 - 2, HX0 + bx + 2), False)
    level1 = Level(l1, 0.25, px * bx1 - HX1, nx // 2, (py * by1, ny // 2),
                   (nz // 2, LANES), (HX1 - 2, HX1 + bx1 + 2), False)
    level2 = Level(l2, 0.25**2, -PAD2, nx // 4, (0, ny // 4), (nz // 4, half),
                   (PAD2, wide2 - PAD2), True)
    level3 = Level(l3, 0.25**3, -1, nx // 8, (0, ny // 8), (nz // 8, half), (1, wide3 - 1), True)
    level2.clear(level2.g, level2.u)
    level3.clear(level3.g, level3.u)

    halo_m0.arrive()
    halo_m0.unpack(m0, HX0, lambda v: 1.0 / v)
    level0.setup()
    halo_f0.arrive()
    halo_f0.unpack(f0, HX0)
    ma_arrive()
    mb_start()
    level0.scale()
    level0.sweep(f0, u0, 1)
    restrict0(lambda x, n: level0.residual(x, n)[:, 0:by], f1)
    halo_f1.pack(f1, HX1)
    halo_f1.start()
    halo_u0.pack(u0, HX0)

    halo_m1.arrive()
    halo_m1.unpack(m1, HX1)
    level1.setup()
    halo_f1.arrive()
    halo_f1.unpack(f1, HX1)
    level1.scale()
    level1.sweep(f1, u1, 1)
    restrict1(lambda x, n: level1.residual(x, n)[:, 0:by1], gf)
    fa_start()
    halo_u1.pack(u1, HX1)

    def spread(gathered, dst):
        n = bx2 // 2
        lane = iota((n * by2, LANES), 1)
        groups = py_count // 2

        def body(p):
            for q in range(groups):
                a, b = gathered[p, q], gathered[p, q + groups]
                first = jnp.where(lane < half, a, pltpu.roll(b, half, 1))
                second = jnp.where(lane < half, pltpu.roll(a, half, 1), b)
                for i in range(n):
                    rows = slice(q * by2, (q + 1) * by2)
                    piece = slice(i * by2, (i + 1) * by2)
                    dst[PAD2 + p * bx2 + i, rows] = first[piece]
                    dst[PAD2 + p * bx2 + n + i, rows] = second[piece]

        loop(0, px_count, body)

    def pair2(get, dst):
        count = wide3 - 2
        rows = l3[0].shape[1]

        def body(i, n):
            pair_slabs(tmp, i, get(PAD2 + 2 * i, 2 * n))

        chunks(0, count, 2 * level2.size, 24, body)
        sums = pair_rows(tmp, count, rows, LANES)
        dst[1 : 1 + count] = dot(sums.reshape(count * rows, LANES), r_pack).reshape(
            count, rows, LANES
        )

    mb_arrive()
    one2 = jnp.ones((PAD2,) + level2.shape, jnp.float32)
    one3 = jnp.ones(level3.shape, jnp.float32)
    m2, m3 = l2[0], l3[0]
    spread(gm, m2)
    m2[0:PAD2] = one2
    m2[wide2 - PAD2 :] = one2
    level2.setup()
    pair2(lambda x, n: m2[pl.ds(x, n)], m3)
    m3[0] = one3
    m3[wide3 - 1] = one3

    inner3 = slice(1, wide3 - 1)
    m3[inner3] = jnp.where(level3.gz < level3.nz, m3[inner3], 1.0)
    level3.setup()

    fa_arrive()
    fb_start()
    halo_u1.start()
    halo_u0.start()
    fb_arrive()
    f2, f3 = l2[5], l3[5]
    spread(gf, f2)

    level2.scale()
    level2.sweep(level2.g, level2.u)
    pair2(level2.residual, f3)

    level3.scale()
    m3[0] = jnp.zeros(level3.shape, jnp.float32)
    m3[wide3 - 1] = jnp.zeros(level3.shape, jnp.float32)
    level3.sweep(f3, level3.u)
    now, later = level3.u, m3
    for _ in range(COARSE - 2):
        level3.sweep(now, later)
        now, later = later, now

    p_pack = matrix(
        (LANES, LANES), lambda k, z: (z // half == k // half) & ((z % half) // 2 == k % half), 1.0
    )
    count3, rows3 = wide3 - 2, l3[0].shape[1]
    e3 = dot(now[1 : 1 + count3].reshape(count3 * rows3, LANES), p_pack)
    add_double(tmp, [e3.reshape(count3, rows3, LANES)], level2.u, PAD2, level2.size)
    zero2 = jnp.zeros((PAD2,) + level2.shape, jnp.float32)
    m2[0:PAD2] = zero2
    m2[wide2 - PAD2 :] = zero2
    level2.u[0:PAD2] = zero2
    level2.u[wide2 - PAD2 :] = zero2
    level2.sweep(level2.u, m2)
    level2.sweep(m2, level2.u)

    full = 2 * level2.shape[0]
    shift = lax.rem(full - py * by2, full)
    near = by2 + HY // 2

    halo_u1.arrive()
    halo_u1.unpack(u1, HX1)

    def fetch(c, n):
        e = [level2.u[px * bx2 + c + j] for j in range(n)]
        e = [jnp.concatenate([one, pltpu.roll(one, half, 1)], 0) for one in e]
        e = [pltpu.roll(one, shift, 0) for one in e]
        for j in range(n):
            pe1[c + j, 0:near] = e[j][0:near]
            pe1[c + j, near : near + HY // 2] = e[j][full - HY // 2 : full]

    chunks(0, wide1 // 2, 2 * level2.size, 32, fetch)
    p_one = matrix((LANES, LANES), lambda k, z: z // 2 == k, 1.0)
    e2 = dot(pe1[...].reshape(-1, LANES), p_one).reshape(pe1.shape)
    add_double(tmp, [e2[:, 0 : y1 // 2]], level1.u, 0, level1.size)
    level1.sweep(u1, m1)
    level1.sweep(m1, u1, 1)

    p_zero = matrix((LANES, nz), lambda k, z: z // 2 == k, 1.0)
    base = HX1 - HX0 // 2
    count = wide0 // 2
    e1 = dot(level1.u[base : base + count].reshape(count * y1, LANES), p_zero)
    pe0[...] = e1.reshape(pe0.shape)
    halo_u0.arrive()
    halo_u0.unpack(u0, HX0)
    parts = [pe0[:, 0 : by1 + HY // 2], pe0[:, y1 - HY // 2 : y1]]
    add_double(tmp, parts, level0.u, 0, level0.size)
    level0.sweep(u0, m0, 1)

    def last(x, n):
        v, rest = level0.change(m0, HX0 + x, n)
        out[pl.ds(x, n)] = (0.2 * v + rest)[:, 0:by]

    chunks(0, bx, level0.size, 24, last)

    for h in all_halos:
        h.sent()
    for done in (ma_sent, mb_sent, fa_sent, fb_sent):
        done()


def per_device(px_count, py_count, source, density):
    bx, by, nz = source.shape
    f32 = jnp.float32
    bx1, by1, bx2, by2 = bx // 2, by // 2, bx // 4, by // 4

    def level(wide, rows, lanes):
        return [pltpu.VMEM((wide, rows, lanes), f32)] * 7

    y0, y1 = by + 2 * HY, by1 + 2 * HY
    wide0, wide1 = bx + 2 * HX0, bx1 + 2 * HX1
    x2, rows2 = bx2 * px_count, by2 * py_count // 2
    ext = pltpu.VMEM(source.shape, f32)

    def halo(hx, pieces, rows, cols, lanes):
        copies = pltpu.SemaphoreType.DMA((2 + 6 * len(pieces),))
        return [
            pltpu.VMEM((2, hx, cols, lanes), f32),
            pltpu.VMEM((2, hx, cols, lanes), f32),
            [pltpu.VMEM((2, rows, w, lanes), f32) for _, w in pieces],
            [pltpu.VMEM((2, rows + 2 * hx, w, lanes), f32) for _, w in pieces],
            copies,
            copies,
        ]

    take = -(-(y1 // 2) // ROWS) * ROWS
    gather = pltpu.VMEM((px_count, py_count, bx2 * by2 // 2, LANES), f32)
    scratch = [
        ext,
        ext,
        level(wide0, y0, nz),
        level(wide1, y1, LANES),
        level(x2 + 2 * PAD2, rows2, LANES),
        level(x2 // 2 + 2, rows2 // 2, LANES),
        pltpu.VMEM((wide0 // 2, y1, nz), f32),
        pltpu.VMEM((wide1 // 2, take, LANES), f32),
        pltpu.VMEM((bx2 * by2, LANES), f32),
        pltpu.VMEM((nz // LANES, max(wide0, wide1, x2) // 2, max(y0, y1, rows2), LANES), f32),
        gather,
        gather,
        pltpu.SemaphoreType.DMA((2,)),
        [
            halo(3, THREE, bx, by, nz),
            halo(2, TWO, bx, by, nz),
            halo(2, TWO, bx, by, nz),
            halo(3, THREE, bx1, by1, LANES),
            halo(2, TWO, bx1, by1, LANES),
            halo(3, THREE, bx1, by1, LANES),
        ],
        pltpu.SemaphoreType.DMA((2 * (py_count - 1),)),
        pltpu.SemaphoreType.DMA((2 * (py_count - 1),)),
        pltpu.SemaphoreType.DMA((2 * (px_count - 1),)),
        pltpu.SemaphoreType.DMA((2 * (px_count - 1),)),
    ]
    return pl.pallas_call(
        functools.partial(kernel, (px_count, py_count)),
        out_shape=jax.ShapeDtypeStruct(source.shape, f32),
        in_specs=[pl.BlockSpec(memory_space=pl.ANY)] * 2,
        out_specs=pl.BlockSpec(memory_space=pltpu.VMEM),
        scratch_shapes=scratch,
        compiler_params=pltpu.CompilerParams(
            collective_id=0, has_side_effects=True, vmem_limit_bytes=56 * 1024 * 1024
        ),
    )(source, density)


def solution(mesh):
    spec = P("px", "py", None)
    return jax.shard_map(
        functools.partial(per_device, mesh.shape["px"], mesh.shape["py"]),
        mesh=mesh,
        in_specs=(spec, spec),
        out_specs=spec,
        check_vma=False,
    )
```

profile of v0, /device:TPU:0, one launch (start us, length us, event | category | flops | bytes accessed | tf_op | source)
XLA Modules:
  0.0 44.0 jit_solution(9691692293685361122)
XLA Ops:
  0.0 42.1 %shard_map.28 = f32[32,16,256]{2,1,0:T(8,128)} custom-call(f32[32,16,256]{2,1,0:T(8,128)} %source.1, f32[32,16,256]{2,1,0:T(8,128)} %density.1), custom_call_target="tpu_custom_call" | custom-call | tf_op jit(solution)/shard_map/pallas_call | solution.py:626
  42.1 1.9 %copy.4 = f32[32,16,256]{2,1,0:T(8,128)} copy(f32[32,16,256]{2,1,0:T(8,128)} %shard_map.28) | data formatting | bytes 1048576
where the time goes:
time: 44.6 us; the launch traced here: 44 us
  Pallas kernels  42.1 us (94%)
  local copies, waits for them, and re-layouts  1.87 us (4%)
    pallas_call x1, Pallas kernels, per_device(): pl.pallas_call(functools.partial(kernel, (px_count, py_count)), out_shape...  42.1 us
    unnamed x1, local copies, waits for them, and re-layouts  1.87 us

commit v1 on v0

--- a/solution.py
+++ b/solution.py
@@ -10,7 +10,8 @@
 COARSE = 8
 LANES = 128
 HX0, HX1, HY, PAD2 = 4, 4, 4, 2
-THREE, TWO = ((0, 2), (2, 1)), ((0, 2),)
+THREE, TWO = ((0, 2, 3), (2, 1, 3)), ((0, 2, 2),)
+THREE0, TWO0 = ((0, 2, 2), (2, 1, 0)), ((0, 2, 1),)
 ROWS = 8
 DIRECTIONS = [(dx, dy) for dx in (-1, 0, 1) for dy in (-1, 0, 1) if (dx, dy) != (0, 0)]
 MESH = pl.DeviceIdType.MESH
@@ -241,7 +242,7 @@
             hx, (bx, by) = self.hx, self.block
             self.xsend[0] = ref[ox : ox + hx, 0:by]
             self.xsend[1] = ref[ox + bx - hx : ox + bx, 0:by]
-            for ysend, (d, w) in zip(self.ysend, self.pieces):
+            for ysend, (d, w, _) in zip(self.ysend, self.pieces):
                 ysend[0] = ref[ox : ox + bx, d : d + w]
                 ysend[1] = ref[ox : ox + bx, by - d - w : by - d]
 
@@ -254,11 +255,15 @@
                     pairs = [(self.xsend.at[side], self.xland.at[1 - side])]
                 else:
                     side = (dy + 1) // 2
-                    own, there, count = ((0, hx + bx, hx), (0, hx, bx), (bx - hx, 0, hx))[dx + 1]
-                    pairs = [
-                        (a.at[side, pl.ds(own, count)], b.at[1 - side, pl.ds(there, count)])
-                        for a, b in zip(self.ysend, self.yland)
-                    ]
+                    pairs = []
+                    for a, b, (_, _, corner) in zip(self.ysend, self.yland, self.pieces):
+                        own, there, count = (
+                            (0, hx + bx, corner), (0, hx, bx), (bx - corner, hx - corner, corner)
+                        )[dx + 1]
+                        if count:
+                            pairs.append(
+                                (a.at[side, pl.ds(own, count)], b.at[1 - side, pl.ds(there, count)])
+                            )
                 copies = []
                 for a, b in pairs:
                     copies.append(pltpu.make_async_remote_copy(
@@ -289,7 +294,7 @@
             hx, (bx, by), rows = self.hx, self.block, ref.shape[1]
             ref[ox - hx : ox, 0:by] = change(self.xland[0])
             ref[ox + bx : ox + bx + hx, 0:by] = change(self.xland[1])
-            for yland, (d, w) in zip(self.yland, self.pieces):
+            for yland, (d, w, _) in zip(self.yland, self.pieces):
                 ref[ox - hx : ox + bx + hx, rows - d - w : rows - d] = change(yland[0])
                 ref[ox - hx : ox + bx + hx, by + d : by + d + w] = change(yland[1])
 
@@ -309,8 +314,8 @@
                     device_id_type=MESH,
                 ))
 
-        def arrive():
-            for k in range(1, count):
+        def arrive(steps=range(1, count)):
+            for k in steps:
                 frm = lax.rem(me + count - k, count)
                 landed = ref.at[px, frm] if axis else ref.at[frm]
                 pltpu.make_async_remote_copy(
@@ -333,9 +338,9 @@
     for c in own_copies:
         c.start()
     block0, block1 = (bx, by), (bx1, by1)
-    halo_m0 = Halo(halos[0], 3, THREE, block0)
-    halo_f0 = Halo(halos[1], 2, TWO, block0)
-    halo_u0 = Halo(halos[2], 2, TWO, block0)
+    halo_m0 = Halo(halos[0], 3, THREE0, block0)
+    halo_f0 = Halo(halos[1], 2, TWO0, block0)
+    halo_u0 = Halo(halos[2], 2, TWO0, block0)
     halo_m1 = Halo(halos[3], 3, THREE, block1)
     halo_f1 = Halo(halos[4], 2, TWO, block1)
     halo_u1 = Halo(halos[5], 3, THREE, block1)
@@ -406,8 +411,20 @@
     ma_start, ma_arrive, ma_sent = along(1, gm, sa, ra, 0)
     fa_start, fa_arrive, fa_sent = along(1, gf, sa, ra, py_count - 1)
     mb_start, mb_arrive, mb_sent = along(0, gm, sb, rb, 0)
-    fb_start, fb_arrive, fb_sent = along(0, gf, sb, rb, px_count - 1)
+    _, fb_arrive, fb_sent = along(0, gf, sb, rb, px_count - 1)
     ma_start()
+
+    def forward(k):
+        block = gf.at[px, lax.rem(py + py_count - k, py_count)]
+        for step in range(1, px_count):
+            pltpu.make_async_remote_copy(
+                src_ref=block,
+                dst_ref=block,
+                send_sem=sb.at[px_count - 1 + step - 1],
+                recv_sem=rb.at[px_count - 1 + step - 1],
+                device_id=(lax.rem(px + step, px_count), py),
+                device_id_type=MESH,
+            ).start()
 
     level0 = Level(l0, 1.0, px * bx - HX0, nx, (py * by, ny), (nz, nz), (HX0 - 2, HX0 + bx + 2), False)
     level1 = Level(l1, 0.25, px * bx1 - HX1, nx // 2, (py * by1, ny // 2),
@@ -417,6 +434,37 @@
     level3 = Level(l3, 0.25**3, -1, nx // 8, (0, ny // 8), (nz // 8, half), (1, wide3 - 1), True)
     level2.clear(level2.g, level2.u)
     level3.clear(level3.g, level3.u)
+
+    def spread(gathered, dst):
+        n = bx2 // 2
+        lane = iota((n * by2, LANES), 1)
+        groups = py_count // 2
+
+        def body(p):
+            for q in range(groups):
+                a, b = gathered[p, q], gathered[p, q + groups]
+                first = jnp.where(lane < half, a, pltpu.roll(b, half, 1))
+                second = jnp.where(lane < half, pltpu.roll(a, half, 1), b)
+                for i in range(n):
+                    rows = slice(q * by2, (q + 1) * by2)
+                    piece = slice(i * by2, (i + 1) * by2)
+                    dst[PAD2 + p * bx2 + i, rows] = first[piece]
+                    dst[PAD2 + p * bx2 + n + i, rows] = second[piece]
+
+        loop(0, px_count, body)
+
+    def pair2(get, dst):
+        count = wide3 - 2
+        rows = l3[0].shape[1]
+
+        def body(i, n):
+            pair_slabs(tmp, i, get(PAD2 + 2 * i, 2 * n))
+
+        chunks(0, count, 2 * level2.size, 24, body)
+        sums = pair_rows(tmp, count, rows, LANES)
+        dst[1 : 1 + count] = dot(sums.reshape(count * rows, LANES), r_pack).reshape(
+            count, rows, LANES
+        )
 
     halo_m0.arrive()
     halo_m0.unpack(m0, HX0, lambda v: 1.0 / v)
@@ -435,45 +483,6 @@
     halo_m1.arrive()
     halo_m1.unpack(m1, HX1)
     level1.setup()
-    halo_f1.arrive()
-    halo_f1.unpack(f1, HX1)
-    level1.scale()
-    level1.sweep(f1, u1, 1)
-    restrict1(lambda x, n: level1.residual(x, n)[:, 0:by1], gf)
-    fa_start()
-    halo_u1.pack(u1, HX1)
-
-    def spread(gathered, dst):
-        n = bx2 // 2
-        lane = iota((n * by2, LANES), 1)
-        groups = py_count // 2
-
-        def body(p):
-            for q in range(groups):
-                a, b = gathered[p, q], gathered[p, q + groups]
-                first = jnp.where(lane < half, a, pltpu.roll(b, half, 1))
-                second = jnp.where(lane < half, pltpu.roll(a, half, 1), b)
-                for i in range(n):
-                    rows = slice(q * by2, (q + 1) * by2)
-                    piece = slice(i * by2, (i + 1) * by2)
-                    dst[PAD2 + p * bx2 + i, rows] = first[piece]
-                    dst[PAD2 + p * bx2 + n + i, rows] = second[piece]
-
-        loop(0, px_count, body)
-
-    def pair2(get, dst):
-        count = wide3 - 2
-        rows = l3[0].shape[1]
-
-        def body(i, n):
-            pair_slabs(tmp, i, get(PAD2 + 2 * i, 2 * n))
-
-        chunks(0, count, 2 * level2.size, 24, body)
-        sums = pair_rows(tmp, count, rows, LANES)
-        dst[1 : 1 + count] = dot(sums.reshape(count * rows, LANES), r_pack).reshape(
-            count, rows, LANES
-        )
-
     mb_arrive()
     one2 = jnp.ones((PAD2,) + level2.shape, jnp.float32)
     one3 = jnp.ones(level3.shape, jnp.float32)
@@ -482,6 +491,14 @@
     m2[0:PAD2] = one2
     m2[wide2 - PAD2 :] = one2
     level2.setup()
+    halo_f1.arrive()
+    halo_f1.unpack(f1, HX1)
+    level1.scale()
+    level1.sweep(f1, u1, 1)
+    restrict1(lambda x, n: level1.residual(x, n)[:, 0:by1], gf)
+    fa_start()
+    forward(0)
+    halo_u1.pack(u1, HX1)
     pair2(lambda x, n: m2[pl.ds(x, n)], m3)
     m3[0] = one3
     m3[wide3 - 1] = one3
@@ -490,8 +507,10 @@
     m3[inner3] = jnp.where(level3.gz < level3.nz, m3[inner3], 1.0)
     level3.setup()
 
-    fa_arrive()
-    fb_start()
+
+    for k in sorted(range(1, py_count), key=lambda k: (min(k, py_count - k), k)):
+        fa_arrive([k])
+        forward(k)
     halo_u1.start()
     halo_u0.start()
     fb_arrive()
@@ -584,12 +603,12 @@
     ext = pltpu.VMEM(source.shape, f32)
 
     def halo(hx, pieces, rows, cols, lanes):
-        copies = pltpu.SemaphoreType.DMA((2 + 6 * len(pieces),))
+        copies = pltpu.SemaphoreType.DMA((2 + sum(6 if c else 2 for _, _, c in pieces),))
         return [
             pltpu.VMEM((2, hx, cols, lanes), f32),
             pltpu.VMEM((2, hx, cols, lanes), f32),
-            [pltpu.VMEM((2, rows, w, lanes), f32) for _, w in pieces],
-            [pltpu.VMEM((2, rows + 2 * hx, w, lanes), f32) for _, w in pieces],
+            [pltpu.VMEM((2, rows, w, lanes), f32) for _, w, _ in pieces],
+            [pltpu.VMEM((2, rows + 2 * hx, w, lanes), f32) for _, w, _ in pieces],
             copies,
             copies,
         ]
@@ -611,9 +630,9 @@
         gather,
         pltpu.SemaphoreType.DMA((2,)),
         [
-            halo(3, THREE, bx, by, nz),
-            halo(2, TWO, bx, by, nz),
-            halo(2, TWO, bx, by, nz),
+            halo(3, THREE0, bx, by, nz),
+            halo(2, TWO0, bx, by, nz),
+            halo(2, TWO0, bx, by, nz),
             halo(3, THREE, bx1, by1, LANES),
             halo(2, TWO, bx1, by1, LANES),
             halo(3, THREE, bx1, by1, LANES),

time: 44.6 us -> 43.5 us (0.975); the launches traced: 44 us -> 43.3 us
  Pallas kernels: 42.1 us -> 41.5 us
    pallas_call x1, Pallas kernels: 42.1 us -> 41.5 us  [per_device(): pl.pallas_call(functools.partial(kernel, (px_count, py_count)), out_shape...]
where the time goes in v1:
time: 43.5 us; the launch traced here: 43.3 us
  Pallas kernels  41.5 us (95%)
  local copies, waits for them, and re-layouts  1.87 us (4%)
    pallas_call x1, Pallas kernels, per_device(): pl.pallas_call(functools.partial(kernel, (px_count, py_count)), out_shape...  41.5 us
    unnamed x1, local copies, waits for them, and re-layouts  1.87 us

profile of v1, /device:TPU:0, one launch (start us, length us, event | category | flops | bytes accessed | tf_op | source)
XLA Modules:
  0.0 43.3 jit_solution(13322888706181989422)
XLA Ops:
  0.0 41.5 %shard_map.28 = f32[32,16,256]{2,1,0:T(8,128)} custom-call(f32[32,16,256]{2,1,0:T(8,128)} %source.1, f32[32,16,256]{2,1,0:T(8,128)} %density.1), custom_call_target="tpu_custom_call" | custom-call | tf_op jit(solution)/shard_map/pallas_call | solution.py:645
  41.5 1.9 %copy.4 = f32[32,16,256]{2,1,0:T(8,128)} copy(f32[32,16,256]{2,1,0:T(8,128)} %shard_map.28) | data formatting | bytes 1048576

commit v2 on v1

--- a/solution.py
+++ b/solution.py
@@ -8,6 +8,7 @@
 from jax.sharding import PartitionSpec as P
 
 COARSE = 8
+OUT_PARTS = 4
 LANES = 128
 HX0, HX1, HY, PAD2 = 4, 4, 4, 2
 THREE, TWO = ((0, 2, 3), (2, 1, 3)), ((0, 2, 2),)
@@ -22,11 +23,18 @@
 
 
 def dot(a, b):
-    return jnp.dot(a, b, precision=lax.Precision.HIGHEST, preferred_element_type=jnp.float32)
+    total = None
+    for _ in range(3):
+        part = a.astype(jnp.bfloat16)
+        a = a - part.astype(jnp.float32)
+        term = jnp.dot(part, b, preferred_element_type=jnp.float32)
+        total = term if total is None else total + term
+    return total
 
 
 def matrix(shape, test, value):
-    return jnp.where(test(iota(shape, 0), iota(shape, 1)), value, 0.0).astype(jnp.float32)
+    chosen = jnp.where(test(iota(shape, 0), iota(shape, 1)), value, 0.0)
+    return chosen.astype(jnp.bfloat16)
 
 
 def loop(low, high, body, unroll=1):
@@ -579,14 +587,22 @@
 
     def last(x, n):
         v, rest = level0.change(m0, HX0 + x, n)
-        out[pl.ds(x, n)] = (0.2 * v + rest)[:, 0:by]
-
-    chunks(0, bx, level0.size, 24, last)
+        den[pl.ds(x, n)] = (0.2 * v + rest)[:, 0:by]
+
+    quarter = bx // OUT_PARTS
+    results = []
+    for part in range(OUT_PARTS):
+        chunks(part * quarter, (part + 1) * quarter, level0.size, 24, last)
+        at = pl.ds(part * quarter, quarter)
+        results.append(pltpu.make_async_copy(den.at[at], out.at[at], copy_sem.at[part]))
+        results[-1].start()
 
     for h in all_halos:
         h.sent()
     for done in (ma_sent, mb_sent, fa_sent, fb_sent):
         done()
+    for copy in results:
+        copy.wait()
 
 
 def per_device(px_count, py_count, source, density):
@@ -628,7 +644,7 @@
         pltpu.VMEM((nz // LANES, max(wide0, wide1, x2) // 2, max(y0, y1, rows2), LANES), f32),
         gather,
         gather,
-        pltpu.SemaphoreType.DMA((2,)),
+        pltpu.SemaphoreType.DMA((OUT_PARTS,)),
         [
             halo(3, THREE0, bx, by, nz),
             halo(2, TWO0, bx, by, nz),
@@ -646,7 +662,7 @@
         functools.partial(kernel, (px_count, py_count)),
         out_shape=jax.ShapeDtypeStruct(source.shape, f32),
         in_specs=[pl.BlockSpec(memory_space=pl.ANY)] * 2,
-        out_specs=pl.BlockSpec(memory_space=pltpu.VMEM),
+        out_specs=pl.BlockSpec(memory_space=pl.ANY),
         scratch_shapes=scratch,
         compiler_params=pltpu.CompilerParams(
             collective_id=0, has_side_effects=True, vmem_limit_bytes=56 * 1024 * 1024

time: 43.5 us -> 42.9 us (0.986)
  Pallas kernels: 41.5 us -> 40.8 us
    pallas_call x1, Pallas kernels: 41.5 us -> 40.8 us  [per_device(): pl.pallas_call(functools.partial(kernel, (px_count, py_count)), out_shape...]
where the time goes in v2:
time: 42.9 us; the launch traced here: 42.7 us
  Pallas kernels  40.8 us (95%)
  local copies, waits for them, and re-layouts  1.87 us (4%)
    pallas_call x1, Pallas kernels, per_device(): pl.pallas_call(functools.partial(kernel, (px_count, py_count)), out_shape...  40.8 us
    unnamed x1, local copies, waits for them, and re-layouts  1.87 us

profile of v2, /device:TPU:0, one launch (start us, length us, event | category | flops | bytes accessed | tf_op | source)
XLA Modules:
  0.0 42.7 jit_solution(4386749478516465949)
XLA Ops:
  0.0 40.8 %shard_map.28 = f32[32,16,256]{2,1,0:T(8,128)} custom-call(f32[32,16,256]{2,1,0:T(8,128)} %source.1, f32[32,16,256]{2,1,0:T(8,128)} %density.1), custom_call_target="tpu_custom_call" | custom-call | tf_op jit(solution)/shard_map/pallas_call | solution.py:661
  40.8 1.9 %copy.4 = f32[32,16,256]{2,1,0:T(8,128)} copy(f32[32,16,256]{2,1,0:T(8,128)} %shard_map.28) | data formatting | bytes 1048576

commit v3 on v2

--- a/solution.py
+++ b/solution.py
@@ -149,8 +149,9 @@
 
     def change(self, ref, x, n):
         at = pl.ds(x, n)
-        v, wy, wz = ref[at], self.wy[at], self.wz[at]
-        total = self.wx[at] * ref[pl.ds(x + 1, n)] + self.wx[pl.ds(x - 1, n)] * ref[pl.ds(x - 1, n)]
+        wide, wx = ref[pl.ds(x - 1, n + 2)], self.wx[pl.ds(x - 1, n + 1)]
+        v, wy, wz = wide[1 : n + 1], self.wy[at], self.wz[at]
+        total = wx[1 : n + 1] * wide[2 : n + 2] + wx[0:n] * wide[0:n]
         total = total + (wy * self.y_plus(v) + self.y_minus(wy * v))
         total = total + (wz * self.z_plus(v) + self.z_minus(wz * v))
         return v, self.g[at] + self.k[at] * total

time: 42.9 us -> 42.8 us (level)
  no operation moved by 1% of the time
where the time goes in v3:
time: 42.8 us; the launch traced here: 42.7 us
  Pallas kernels  40.8 us (95%)
  local copies, waits for them, and re-layouts  1.87 us (4%)
    pallas_call x1, Pallas kernels, per_device(): pl.pallas_call(functools.partial(kernel, (px_count, py_count)), out_shape...  40.8 us
    unnamed x1, local copies, waits for them, and re-layouts  1.87 us

profile of v3, /device:TPU:0, one launch (start us, length us, event | category | flops | bytes accessed | tf_op | source)
XLA Modules:
  0.0 42.7 jit_solution(12345137257137443700)
XLA Ops:
  0.0 40.8 %shard_map.28 = f32[32,16,256]{2,1,0:T(8,128)} custom-call(f32[32,16,256]{2,1,0:T(8,128)} %source.1, f32[32,16,256]{2,1,0:T(8,128)} %density.1), custom_call_target="tpu_custom_call" | custom-call | tf_op jit(solution)/shard_map/pallas_call | solution.py:662
  40.8 1.9 %copy.4 = f32[32,16,256]{2,1,0:T(8,128)} copy(f32[32,16,256]{2,1,0:T(8,128)} %shard_map.28) | data formatting | bytes 1048576
